TPU v7x, 256 devices: a whole 4x4x8 slice. The times are simulated.
256 devices in a mesh: tp: 8 (over z_lo, x), ep: 32 (over y, z_hi, core).
Axes of the slice: x: 4, y: 4, z: 8 (z_hi: 4, z_lo: 2; z = z_hi * 2 + z_lo), core: 2. Of those that a mesh axis runs over, the one named last changes fastest.
Arguments:
- tokens: bfloat16 [6144, 4096], P('ep', 'tp'), may hold values from -6 to 6
- routes: int32 [6144, 2], P('ep'), may hold values from 0 to 31, all different within a row; in each aligned block of 192 rows (0 to 191, 192 to 383, ...) at most 24 rows name the same one
- combine: float32 [6144, 2], P('ep'), may hold values from 0.2 to 1
- expert_slot: int32 [32], replicated, may hold values from 0 to 31, each once
- dense_gate: bfloat16 [4096, 3072], P('ep', 'tp'), may hold values from -0.09375 to 0.09375
- dense_up: bfloat16 [4096, 3072], P('ep', 'tp'), may hold values from -0.09375 to 0.09375
- dense_down: bfloat16 [3072, 4096], P('tp', 'ep'), may hold values from -0.109375 to 0.109375
- expert_gate: bfloat16 [32, 4096, 3072], P('ep', None, 'tp'), may hold values from -0.09375 to 0.09375
- expert_up: bfloat16 [32, 4096, 3072], P('ep', None, 'tp'), may hold values from -0.09375 to 0.09375
- expert_down: bfloat16 [32, 3072, 4096], P('ep', 'tp'), may hold values from -0.109375 to 0.109375
Outputs:
- mixed: bfloat16 [6144, 4096], P('ep', 'tp')
Inputs may be any that keep to these rules, and one draw needn't show every extreme that they name: `routes`: the two experts of a row differ. In each aligned block of 192 rows no expert is named by more than 24 rows, and in every draw some expert is named by exactly 24 rows of some block. A permutation: expert e uses block expert_slot[e] of expert_gate, expert_up and expert_down.
All inputs are finite; a program needn't handle non-finite values.
Results may differ from a plain program's by a relative error of at most 0.015.
Values may be sent and summed in bfloat16 or wider, within the bound.
A program may use at most 128 MiB of HBM per device.

v0:
```python
import jax
import jax.numpy as jnp
from jax import lax
from jax.sharding import PartitionSpec as P


def swiglu_hidden(gate, up):
    return (jax.nn.silu(gate) * up).astype(jnp.bfloat16)


def body(
    tokens,
    routes,
    combine,
    expert_slot,
    dense_gate,
    dense_up,
    dense_down,
    expert_gate,
    expert_up,
    expert_down,
):
    n_ep = lax.axis_size("ep")
    tok_rows = tokens.shape[0]
    slice_width = tokens.shape[1]
    capacity = 4 * tok_rows // n_ep
    whole = lax.all_gather(tokens, "tp", axis=1, tiled=True)
    width = whole.shape[1]
    gate_next = jnp.dot(
        whole,
        lax.all_gather(dense_gate, "ep", axis=0, tiled=True),
        preferred_element_type=jnp.float32,
    )
    up_next = jnp.dot(
        whole,
        lax.all_gather(dense_up, "ep", axis=0, tiled=True),
        preferred_element_type=jnp.float32,
    )
    dense_hidden = swiglu_hidden(gate_next, up_next)
    dense_terms = jnp.dot(
        dense_hidden,
        lax.all_gather(dense_down, "ep", axis=1, tiled=True),
        preferred_element_type=jnp.float32,
    )
    dense_out = lax.psum_scatter(
        dense_terms.astype(jnp.bfloat16), "tp", scatter_dimension=1, tiled=True
    ).astype(jnp.float32)
    flat_ids = routes.reshape(-1)
    experts = expert_slot.shape[0]
    onehot = (flat_ids[:, None] == jnp.arange(experts, dtype=jnp.int32)[None, :]).astype(jnp.int32)
    dest = jnp.sum(onehot * expert_slot[None, :], axis=1)
    rank = jnp.cumsum(onehot, axis=0) - 1
    pos = jnp.sum(onehot * rank, axis=1)
    slot_index = dest * capacity + pos
    token_of = jnp.arange(2 * tok_rows, dtype=jnp.int32) // 2
    table = jnp.full((n_ep * capacity,), tok_rows, jnp.int32).at[slot_index].set(token_of)
    gate_w = expert_gate[0]
    up_w = expert_up[0]
    buffer_rows = n_ep * capacity
    source = jnp.concatenate([whole, jnp.zeros((1, width), whole.dtype)], axis=0)
    outgoing = source[table].reshape(n_ep, capacity, width)
    arrived = lax.all_to_all(outgoing, "ep", split_axis=0, concat_axis=0, tiled=True).reshape(
        buffer_rows, width
    )
    expert_g = jnp.dot(arrived, gate_w, preferred_element_type=jnp.float32)
    expert_u = jnp.dot(arrived, up_w, preferred_element_type=jnp.float32)
    expert_hidden = swiglu_hidden(expert_g, expert_u)
    expert_terms = jnp.dot(expert_hidden, expert_down[0], preferred_element_type=jnp.float32)
    expert_sum = lax.psum_scatter(
        expert_terms.astype(jnp.bfloat16), "tp", scatter_dimension=1, tiled=True
    )
    expert_out = expert_sum.reshape(n_ep, capacity, slice_width)
    returned = lax.all_to_all(expert_out, "ep", split_axis=0, concat_axis=0, tiled=True).reshape(
        buffer_rows, slice_width
    )
    picked = returned[slot_index].reshape(tok_rows, 2, slice_width).astype(jnp.float32)
    expert_mix = jnp.sum(picked * combine[:, :, None], axis=1)
    total = tokens.astype(jnp.float32) + dense_out + expert_mix
    return total.astype(jnp.bfloat16)


def solution(mesh):
    in_specs = (
        P("ep", "tp"),
        P("ep", None),
        P("ep", None),
        P(),
        P("ep", "tp"),
        P("ep", "tp"),
        P("tp", "ep"),
        P("ep", None, "tp"),
        P("ep", None, "tp"),
        P("ep", "tp", None),
    )
    out_specs = P("ep", "tp")
    return jax.shard_map(body, mesh=mesh, in_specs=in_specs, out_specs=out_specs, check_vma=False)
```

profile of v0, /device:TPU:1, one launch (start us, length us, event | category | flops | bytes accessed | tf_op | source)
XLA Modules:
  0.0 466.1 jit_solution(9448173665798948665)
XLA Ops:
  6.5 0.7 all-gather.5.cloned.1.call-update
  7.3 0.7 all-gather.7.cloned.1.call-update
  8.0 0.8 copy.12
  8.8 0.1 eq.29
  9.1 0.9 reduce-window.6
  10.0 0.2 slice_reduce_fusion
  10.3 0.8 select_reduce_fusion
  11.1 2.9 scatter_custom_fusion
  14.0 36.0 %all-gather.5.cloned.1.call-done = bf16[192,4096]{1,0:T(8,128)(2,1)} async-done(((bf16[192,512]{1,0:T(8,128)(2,1)}), bf16[192,4096]{1,0:T(8,128)(2,1)}) %all-gather.5.cloned.1.call-update) | async-done | bytes 1572880 | tf_op jit(solution)/shard_map/all_gather | solution.py:27
  50.0 2.8 concatenate.3
  52.7 13.6 %gather_fusion = bf16[768,4096]{1,0:T(8,128)(2,1)} fusion(bf16[193,4096]{1,0:T(8,128)(2,1)} %concatenate.3, s32[1024]{0:T(1024)S(1)} %pad_clamp_fusion.1), kind=kCustom, calls=%fused_computation | custom fusion | bytes 12585984 | tf_op jit(solution)/shard_map/gather | solution.py:61
  66.3 15.6 %all-to-all-start = ((bf16[32,24,4096]{2,1,0:T(8,128)(2,1)}), bf16[32,24,4096]{2,1,0:T(8,128)(2,1)}, u32[]{:S(2)}, u32[]{:S(2)}) async-start(bf16[32,24,4096]{2,1,0:T(8,128)(2,1)} %bitcast.42), calls=%async_computation.1 | async-start | bytes 12582912 | tf_op jit(solution)/shard_map/all_to_all | solution.py:62
  82.0 0.7 all-gather.9.cloned.1.call-update
  82.7 0.5 all-gather.11.cloned.1.call-update
  83.3 122.6 %all-to-all-done = bf16[32,24,4096]{2,1,0:T(8,128)(2,1)} async-done(((bf16[32,24,4096]{2,1,0:T(8,128)(2,1)}), bf16[32,24,4096]{2,1,0:T(8,128)(2,1)}, u32[]{:S(2)}, u32[]{:S(2)}) %all-to-all-start) | async-done | bytes 6291488 | tf_op jit(solution)/shard_map/all_to_all | solution.py:62
  205.9 6.6 %fusion.3 = f32[768,384]{1,0:T(8,128)S(1)} fusion(bf16[768,4096]{1,0:T(8,128)(2,1)} %bitcast.2, bf16[1,4096,384]{2,1,0:T(8,128)(2,1)} %param.17), kind=kOutput, calls=%fused_computation.8 | convolution fusion | flops 2415919104 | bytes 10616832 | tf_op jit(solution)/shard_map/dot_general | solution.py:65
  212.5 6.3 %fusion.8 = bf16[768,384]{1,0:T(8,128)(2,1)S(1)} fusion(bf16[768,4096]{1,0:T(8,128)(2,1)} %bitcast.2, bf16[1,4096,384]{2,1,0:T(8,128)(2,1)S(1)} %copy-done.2, f32[768,384]{1,0:T(8,128)S(1)} %fusion.3), kind=kOutput, calls=%fused_computation.11 | convolution fusion | flops 2417688576 | bytes 11206656 | tf_op jit(solution)/shard_map/dot_general | solution.py:66
  218.8 5.3 %convolution_convert_fusion = bf16[768,4096]{1,0:T(8,128)(2,1)} fusion(bf16[768,384]{1,0:T(8,128)(2,1)S(1)} %fusion.8, bf16[1,384,4096]{2,1,0:T(8,128)(2,1)S(1)} %copy-done), kind=kOutput, calls=%fused_computation.3 | convolution fusion | flops 2419064832 | bytes 10027008 | tf_op jit(solution)/shard_map/dot_general | solution.py:68
  224.2 0.2 reduce-scatter.3.cloned.1.call-start
  224.4 3.3 fusion.28
  227.8 44.8 %all-gather.9.cloned.1.call-done = bf16[4096,384]{1,0:T(8,128)(2,1)} async-done(((bf16[128,384]{1,0:T(8,128)(2,1)}), bf16[4096,384]{1,0:T(8,128)(2,1)}) %all-gather.9.cloned.1.call-update) | async-done | bytes 3145744 | tf_op jit(solution)/shard_map/all_gather | solution.py:36
  272.5 59.9 %all-gather.11.cloned.1.call-done = bf16[384,4096]{1,0:T(8,128)(2,1)} async-done(((bf16[384,128]{1,0:T(8,128)(2,1)}), bf16[384,4096]{1,0:T(8,128)(2,1)}) %all-gather.11.cloned.1.call-update) | async-done | bytes 3145744 | tf_op jit(solution)/shard_map/all_gather | solution.py:42
  332.5 6.4 %convolution_convert_fusion.1 = bf16[192,4096]{1,0:T(8,128)(2,1)} fusion(bf16[384,4096]{1,0:T(8,128)(2,1)} %all-gather.11.cloned.1.call-done, bf16[192,4096]{1,0:T(8,128)(2,1)} %all-gather.5.cloned.1.call-done, bf16[4096,384]{1,0:T(8,128)(2,1)} %all-gather.9.cloned.1.call-done, f32[192,384]{1,0:T(8,128)S(1)} %fusion.28), kind=kOutput, calls=%fused_computation.4 | convolution fusion | flops 1209188352 | bytes 9732096 | tf_op jit(solution)/shard_map/dot_general | solution.py:40
  338.9 69.2 %reduce-scatter.5.cloned.1.call-done = bf16[768,512]{1,0:T(8,128)(2,1)} async-done(((bf16[768,4096]{1,0:T(8,128)(2,1)}), bf16[768,512]{1,0:T(8,128)(2,1)}) %reduce-scatter.5.cloned.1.call-update) | async-done | bytes 786448 | tf_op jit(solution)/shard_map/reduce_scatter | solution.py:69
  408.0 9.4 %all-to-all-start.1 = ((bf16[32,24,512]{2,1,0:T(8,128)(2,1)}), bf16[32,24,512]{2,1,0:T(8,128)(2,1)}, u32[]{:S(2)}, u32[]{:S(2)}) async-start(bf16[32,24,512]{2,1,0:T(8,128)(2,1)} %bitcast.43), calls=%async_computation.3 | async-start | bytes 1572864 | tf_op jit(solution)/shard_map/all_to_all | solution.py:73
  417.4 0.8 copy.15
  418.2 29.4 %all-to-all-done.1 = bf16[32,24,512]{2,1,0:T(8,128)(2,1)} async-done(((bf16[32,24,512]{2,1,0:T(8,128)(2,1)}), bf16[32,24,512]{2,1,0:T(8,128)(2,1)}, u32[]{:S(2)}, u32[]{:S(2)}) %all-to-all-start.1) | async-done | bytes 786464 | tf_op jit(solution)/shard_map/all_to_all | solution.py:73
  447.6 3.3 gather_fusion.1
  450.9 1.4 reshape.67
  452.3 2.2 multiply_reduce_fusion
  454.5 3.0 reduce-scatter.3.cloned.1.call-done
  457.5 1.8 add_convert_fusion
  (23 shorter events, 0.5 us)
Async XLA Ops:
  6.5 212.3 %copy-start = (bf16[1,384,4096]{2,1,0:T(8,128)(2,1)S(1)}, bf16[1,384,4096]{2,1,0:T(8,128)(2,1)}, u32[]{:S(2)}) copy-start(bf16[1,384,4096]{2,1,0:T(8,128)(2,1)} %param.19) | copy-start | bytes 9437188
  6.5 43.4 %all-gather.5.cloned.1.call-start = ((), (), s32[]{:S(2)}) async-start(), calls=%async_computation.4 | async-start | bytes 1769472 | tf_op jit(solution)/shard_map/all_gather | solution.py:27
  7.3 217.1 %all-gather.7.cloned.1.call-start = ((), (), s32[]{:S(2)}) async-start(), calls=%async_computation.5 | async-start | bytes 3244032 | tf_op jit(solution)/shard_map/all_gather | solution.py:31
  66.3 139.6 %all-to-all-start = ((bf16[32,24,4096]{2,1,0:T(8,128)(2,1)}), bf16[32,24,4096]{2,1,0:T(8,128)(2,1)}, u32[]{:S(2)}, u32[]{:S(2)}) async-start(bf16[32,24,4096]{2,1,0:T(8,128)(2,1)} %bitcast.42), calls=%async_computation.1 | async-start | bytes 12582912 | tf_op jit(solution)/shard_map/all_to_all | solution.py:62
  81.9 190.6 %all-gather.9.cloned.1.call-start = ((), (), s32[]{:S(2)}) async-start(), calls=%async_computation.6 | async-start | bytes 3244032 | tf_op jit(solution)/shard_map/all_gather | solution.py:36
  82.7 249.8 %all-gather.11.cloned.1.call-start = ((), (), s32[]{:S(2)}) async-start(), calls=%async_computation.7 | async-start | bytes 3244032 | tf_op jit(solution)/shard_map/all_gather | solution.py:42
  83.2 324.8 %reduce-scatter.5.cloned.1.call-start = ((), (), s32[]{:S(2)}) async-start(), calls=%async_computation.9 | async-start | bytes 7077888 | tf_op jit(solution)/shard_map/reduce_scatter | solution.py:69
  205.9 6.6 %copy-start.2 = (bf16[1,4096,384]{2,1,0:T(8,128)(2,1)S(1)}, bf16[1,4096,384]{2,1,0:T(8,128)(2,1)}, u32[]{:S(2)}) copy-start(bf16[1,4096,384]{2,1,0:T(8,128)(2,1)} %param.18) | copy-start | bytes 9437188
  224.2 233.3 %reduce-scatter.3.cloned.1.call-start = ((), (), s32[]{:S(2)}) async-start(), calls=%async_computation.8 | async-start | bytes 1769472 | tf_op jit(solution)/shard_map/reduce_scatter | solution.py:45
  338.8 78.6 %copy-start.1 = (f32[192,2]{0,1:T(2,128)S(1)}, f32[192,2]{0,1:T(2,128)}, u32[]{:S(2)}) copy-start(f32[192,2]{0,1:T(2,128)} %param.12) | copy-start | bytes 4612
  408.0 39.6 %all-to-all-start.1 = ((bf16[32,24,512]{2,1,0:T(8,128)(2,1)}), bf16[32,24,512]{2,1,0:T(8,128)(2,1)}, u32[]{:S(2)}, u32[]{:S(2)}) async-start(bf16[32,24,512]{2,1,0:T(8,128)(2,1)} %bitcast.43), calls=%async_computation.3 | async-start | bytes 1572864 | tf_op jit(solution)/shard_map/all_to_all | solution.py:73
Sparse Core Ops, SparseCore 0:
  9.2 40.7 all-gather.4
  52.5 84.9 all-gather.6
  140.0 132.4 all-gather.8
  274.9 57.5 all-gather.10
  334.9 73.1 reduce-scatter.4
  410.4 46.9 reduce-scatter.2
where the time goes:
time: 468 us; the launch traced here: 466 us
  waiting for transfers between devices  368 us (79%)
  matrix products  27.9 us (6%)
  local copies, waits for them, and re-layouts  26.1 us (6%)
  starting transfers between devices  25.3 us (5%)
  between operations  13.6 us (3%)
  other arithmetic  5.67 us (1%)
    all_to_all x1, waiting for transfers between devices, body(): lax.all_to_all(outgoing, 'ep', split_axis=0, concat_axis=0, tiled=True)  123 us
    reduce_scatter x1, waiting for transfers between devices, body(): lax.psum_scatter(expert_terms.astype(jnp.bfloat16), 'tp', scatter_dimensi...  69.2 us
    all_gather x1, waiting for transfers between devices, body(): lax.all_gather(dense_down, 'ep', axis=1, tiled=True)  59.9 us
    all_gather x1, waiting for transfers between devices, body(): lax.all_gather(dense_up, 'ep', axis=0, tiled=True)  44.8 us
    all_gather x1, waiting for transfers between devices, body(): whole = lax.all_gather(tokens, 'tp', axis=1, tiled=True)  36 us
    all_to_all x1, waiting for transfers between devices, body(): lax.all_to_all(expert_out, 'ep', split_axis=0, concat_axis=0, tiled=True)  29.4 us
    all_to_all x1, starting transfers between devices, body(): lax.all_to_all(outgoing, 'ep', split_axis=0, concat_axis=0, tiled=True)  15.6 us
    gather x1, local copies, waits for them, and re-layouts, body(): outgoing = source[table].reshape(n_ep, capacity, width)  13.6 us
  transfers between devices with their start and end apart: 8, of which 7 were waited for; matrix products, arithmetic and copies ran while one was open for 12% of the time, Pallas kernels for 0%

commit v1 on v0

v1 whole, which is shorter than its diff:
```python
import jax
import jax.numpy as jnp
from jax import lax
from jax.experimental import pallas as pl
from jax.experimental.pallas import tpu as pltpu
from jax.sharding import PartitionSpec as P

MESH = pl.DeviceIdType.MESH
BF16 = jnp.bfloat16
F32 = jnp.float32

NR = 4
NZL = 2
CAP = 24
PAIR = 2 * CAP
ROWS = NR * NR * PAIR
CH = NR * PAIR
HALF = CH // 2
N_SEM = 160

A2A, META, TOK, INFO, AG, WZ, WY, WS, RS, RET, SIB = 0, 16, 32, 33, 34, 70, 74, 90, 106, 142, 158


def dot(a, b):
    return jnp.dot(a, b, preferred_element_type=F32)


def dot_nt(a, b):
    return lax.dot_general(a, b, (((1,), (1,)), ((), ())), preferred_element_type=F32)


def silu(v):
    return v / (1.0 + jnp.exp(-v))


def kernel(
    tokens,
    routes,
    combine,
    slots,
    dense_gate,
    dense_up,
    dense_down,
    expert_gate,
    expert_up,
    expert_down,
    out,
    tok,
    info,
    meta_out,
    meta_in,
    scale_e,
    scale_d,
    w_gate,
    w_up,
    w_down,
    w_all,
    outgoing,
    x_all,
    acc_g,
    acc_u,
    hidden,
    rs_send,
    rs_half,
    rs_full,
    rs_z,
    result,
    returned,
    part_send,
    part_recv,
    part_own,
    send_sem,
    recv_sem,
    load_sem,
):
    n_tok, width = tokens.shape
    ff = w_gate.shape[1]
    piece = dense_gate.shape[0]
    tp = lax.axis_index("tp")
    ep = lax.axis_index("ep")
    x, zl = tp % NR, tp // NR
    core, zh, y = ep % 2, (ep // 2) % NR, ep // (2 * NR)

    def at_x(d):
        return {"tp": zl * NR + (x + d + NR) % NR, "ep": ep}

    def at_chip(dy, dz):
        return {"tp": tp, "ep": ((y + dy + NR) % NR) * (2 * NR) + ((zh + dz + NR) % NR) * 2 + core}

    partner = {"tp": (1 - zl) * NR + x, "ep": ep}
    sibling = {"tp": tp, "ep": ep + 1 - 2 * core}

    sent = {}

    def send(number, src, dst, device):
        copy = pltpu.make_async_remote_copy(
            src_ref=src,
            dst_ref=dst,
            send_sem=send_sem.at[number],
            recv_sem=recv_sem.at[number],
            device_id=device,
            device_id_type=MESH,
        )
        copy.start()
        sent[number] = copy

    def arrived(number):
        sent[number].wait_recv()

    loads = []

    def load(src, dst):
        copy = pltpu.make_async_copy(src, dst, load_sem.at[len(loads)])
        copy.start()
        loads.append(copy)

    load(tokens, tok.at[core])
    load(dense_gate, w_all.at[0, 0])
    load(dense_up, w_all.at[0, 1])
    for j in range(ff // 128):
        load(dense_down.at[pl.ds(128 * j, 128), :], w_all.at[0, 2, :, pl.ds(128 * j, 128)])
    n_dense = len(loads)
    load(expert_gate.at[0], w_gate)
    load(expert_up.at[0], w_up)
    load(expert_down.at[0], w_down)

    peers = [partner, sibling, at_x(1), at_x(-1)]
    peers += [at_chip(dy, dz) for dz in range(NR) for dy in range(NR) if dy or dz]
    barrier = pltpu.get_barrier_semaphore()
    for peer in peers:
        pl.semaphore_signal(barrier, inc=1, device_id=peer, device_id_type=MESH)

    route = routes[...]
    lanes = lax.broadcasted_iota(jnp.int32, (n_tok, slots.shape[1]), 1)
    picks = [(route[:, k : k + 1] == lanes).astype(F32) for k in range(2)]
    row_id = lax.broadcasted_iota(jnp.int32, (n_tok, n_tok), 0)
    col_id = lax.broadcasted_iota(jnp.int32, (n_tok, n_tok), 1)
    before = (col_id < row_id).astype(BF16)
    eye = (col_id == row_id).astype(F32)
    earlier = dot(before, (picks[0] + picks[1]).astype(BF16))
    slot_row = slots[...].astype(F32)
    columns = []
    for k in range(2):
        pos = jnp.sum(picks[k] * earlier, axis=1, keepdims=True).astype(jnp.int32)
        dest = jnp.sum(picks[k] * slot_row, axis=1, keepdims=True).astype(jnp.int32)
        rel_z = (zh - ((dest >> 1) & (NR - 1)) + NR) & (NR - 1)
        rel_y = (y - (dest >> 3) + NR) & (NR - 1)
        place = (dest & 1) * ROWS + (rel_z * NR + rel_y) * PAIR + core * CAP + pos
        columns.append(place.astype(F32))
    for k in range(2):
        columns.append(combine[:, k : k + 1])
    for number, column in enumerate(columns):
        info[core, number : number + 1, :] = jnp.sum(eye * column, axis=0, keepdims=True)

    pl.semaphore_wait(barrier, len(peers))
    loads[0].wait()
    send(TOK, tok.at[core], tok.at[core], sibling)
    send(INFO, info.at[core], info.at[core], sibling)
    for copy in loads[1:n_dense]:
        copy.wait()

    def w_slot(dz, dy, dc):
        return (dz * NR + dy) * 2 + dc

    hp = piece // 2

    def w_send(number, slot, target, device, half=None):
        if half is None:
            send(number, w_all.at[slot], w_all.at[target], device)
        else:
            rows = pl.ds(half * hp, hp)
            send(number, w_all.at[slot, :, rows, :], w_all.at[target, :, rows, :], device)

    def w_spread(dz):
        slot = w_slot(dz, 0, 0)
        w_send(WY + 4 * dz, slot, w_slot(dz, 3, 0), at_chip(1, 0))
        w_send(WY + 4 * dz + 1, slot, w_slot(dz, 1, 0), at_chip(-1, 0))

    def w_sibling(dz, dy):
        w_send(WS + dz * NR + dy, w_slot(dz, dy, 0), w_slot(dz, dy, 1), sibling)

    def w_across(dz):
        arrived(WY + 4 * dz)
        w_send(WY + 4 * dz + 2, w_slot(dz, 3, 0), w_slot(dz, 2, 0), at_chip(1, 0), 0)
        arrived(WY + 4 * dz + 1)
        w_send(WY + 4 * dz + 3, w_slot(dz, 1, 0), w_slot(dz, 2, 0), at_chip(-1, 0), 1)
        w_sibling(dz, 3)
        w_sibling(dz, 1)

    def w_last(dz):
        arrived(WY + 4 * dz + 2)
        arrived(WY + 4 * dz + 3)
        w_sibling(dz, 2)

    def w0():
        w_spread(0)
        w_send(WZ, w_slot(0, 0, 0), w_slot(3, 0, 0), at_chip(0, 1))
        w_send(WZ + 1, w_slot(0, 0, 0), w_slot(1, 0, 0), at_chip(0, -1))
        w_sibling(0, 0)

    def w1():
        arrived(WZ)
        w_send(WZ + 2, w_slot(3, 0, 0), w_slot(2, 0, 0), at_chip(0, 1), 0)
        arrived(WZ + 1)
        w_send(WZ + 3, w_slot(1, 0, 0), w_slot(2, 0, 0), at_chip(0, -1), 1)
        w_spread(3)
        w_spread(1)
        w_sibling(3, 0)
        w_sibling(1, 0)
        w_across(0)

    def w2():
        arrived(WZ + 2)
        arrived(WZ + 3)
        w_spread(2)
        w_sibling(2, 0)
        w_last(0)
        w_across(3)
        w_across(1)

    def w3():
        w_across(2)
        w_last(3)
        w_last(1)

    def w4():
        w_last(2)

    def w5():
        for number in range(NR * NR):
            arrived(WS + number)

    arrived(TOK)
    arrived(INFO)
    place = [
        jnp.concatenate([info[b, k : k + 1, :] for b in range(2)], axis=1).astype(jnp.int32) - core * ROWS
        for k in range(2)
    ]
    weight = [jnp.concatenate([info[b, 2 + k : 3 + k, :] for b in range(2)], axis=1) for k in range(2)]
    both = jnp.concatenate([tok[0], tok[1]], axis=0)
    zero_row = jnp.zeros((1, 2 * n_tok), F32)
    tables = []
    for k in range(2):
        high = weight[k].astype(BF16).astype(F32)
        rest = weight[k] - high
        middle = rest.astype(BF16).astype(F32)
        low = rest - middle
        first = zero_row + (1.0 - k)
        tables.append(jnp.concatenate([high, middle, low, first] + [zero_row] * 4, axis=0).astype(BF16))

    for g in range(NR):
        rows = lax.broadcasted_iota(jnp.int32, (CH, 2 * n_tok), 0) + g * CH
        picks = [(place[k] == rows).astype(F32) for k in range(2)]
        block = dot((picks[0] + picks[1]).astype(BF16), both).astype(BF16)
        marks = dot_nt(tables[0], picks[0].astype(BF16)) + dot_nt(tables[1], picks[1].astype(BF16))
        for dy in range(NR):
            n = g * NR + dy
            mark = marks[:, dy * PAIR : (dy + 1) * PAIR]
            if n == 0:
                x_all[0, 0:PAIR, :] = block[0:PAIR]
                meta_in[0, :, 0:PAIR] = mark
            else:
                meta_out[n, :, 0:PAIR] = mark
        if g == 0:
            outgoing[PAIR:CH, :] = block[PAIR:CH]
        else:
            outgoing[g * CH : (g + 1) * CH, :] = block
        for dy in range(NR):
            n = g * NR + dy
            if n:
                span = pl.ds(n * PAIR, PAIR)
                send(A2A + n, outgoing.at[span, :], x_all.at[0, span, :], at_chip(-dy, -g))
                send(META + n, meta_out.at[n], meta_in.at[n], at_chip(-dy, -g))

    w0()

    def ag_send(g, number, slot, target, device, half=None):
        if half is None:
            rows = pl.ds(g * CH, CH)
        else:
            rows = pl.ds(g * CH + half * HALF, HALF)
        send(AG + 9 * g + number, x_all.at[slot, rows, :], x_all.at[target, rows, :], device)

    def ag_arrived(g, number):
        arrived(AG + 9 * g + number)

    def s1(g):
        for dy in range(NR):
            if g * NR + dy:
                arrived(A2A + g * NR + dy)
        ag_send(g, 0, 0, 4, partner)
        ag_send(g, 1, 0, 3, at_x(1))
        ag_send(g, 2, 0, 1, at_x(-1))

    def s2(g):
        ag_arrived(g, 0)
        ag_send(g, 3, 4, 7, at_x(1))
        ag_send(g, 4, 4, 5, at_x(-1))
        ag_arrived(g, 1)
        ag_send(g, 5, 3, 2, at_x(1), 0)
        ag_arrived(g, 2)
        ag_send(g, 6, 1, 2, at_x(-1), 1)

    def s3(g):
        ag_arrived(g, 3)
        ag_send(g, 7, 7, 6, at_x(1), 0)
        ag_arrived(g, 4)
        ag_send(g, 8, 5, 6, at_x(-1), 1)

    def tp_of(slot):
        return ((zl + slot // NR) % NZL) * NR + (x + slot % NR) % NR

    def dense_slots(t):
        found = []
        for j in range(4):
            e = t * 4 + j
            dz = ((e // 2) % NR - zh + NR) % NR
            dy = (e // (2 * NR) - y + NR) % NR
            dc = (j % 2 + core) % 2
            found.append(w_slot(dz, dy, dc))
        return found

    def s4(g):
        for number in range(5, 9):
            ag_arrived(g, number)
        acc_g[g] = jnp.zeros((CH, ff), F32)
        acc_u[g] = jnp.zeros((CH, ff), F32)

        def step(slot, _):
            part = x_all[slot, pl.ds(g * CH, CH), :]
            rows = pl.ds(pl.multiple_of(tp_of(slot) * width, width), width)
            acc_g[g] += dot(part, w_gate[rows, :])
            acc_u[g] += dot(part, w_up[rows, :])
            return 0

        lax.fori_loop(0, NZL * NR, step, 0)
        spread = jnp.concatenate([scale_e[g * CH : (g + 1) * CH, :]] * (ff // 128), axis=1)
        hidden[g, :, 0:ff] = (silu(acc_g[g]) * acc_u[g] * spread).astype(BF16)

    def dense(g):
        acc_g[g] = jnp.zeros((CH, ff), F32)
        acc_u[g] = jnp.zeros((CH, ff), F32)

        def step(slot, _):
            part = x_all[slot, pl.ds(g * CH, CH), :]
            found = dense_slots(tp_of(slot))
            acc_g[g] += dot(part, jnp.concatenate([w_all[s, 0] for s in found], axis=0))
            acc_u[g] += dot(part, jnp.concatenate([w_all[s, 1] for s in found], axis=0))
            return 0

        lax.fori_loop(0, NZL * NR, step, 0)
        spread = jnp.concatenate([scale_d[g * CH : (g + 1) * CH, :]] * (ff // 128), axis=1)
        hidden[g, :, ff : 2 * ff] = (silu(acc_g[g]) * acc_u[g] * spread).astype(BF16)

    def scales():
        pick = lax.broadcasted_iota(jnp.int32, (PAIR, 128), 0) == lax.broadcasted_iota(jnp.int32, (PAIR, 128), 1)
        for n in range(NR * NR):
            if n:
                arrived(META + n)
            mark = meta_in[n]
            value = mark[0:1] + mark[1:2] + mark[2:3]
            first = mark[3:4]
            for row, target in ((value, scale_e), (first, scale_d)):
                column = jnp.sum(jnp.where(pick, row, 0.0), axis=1, keepdims=True)
                target[n * PAIR : (n + 1) * PAIR, :] = jnp.broadcast_to(column, (PAIR, 128))

    s1(0)
    s1(1)
    s2(0)
    w1()
    s1(3)
    s2(1)
    s3(0)
    scales()
    for copy in loads[n_dense:]:
        copy.wait()
    w2()
    s1(2)
    s2(3)
    s3(1)
    s4(0)
    w3()
    s2(2)
    s3(3)
    s4(1)
    w4()
    s3(2)
    s4(3)
    s4(2)
    w5()

    def down(g, dz, dx):
        t = ((zl + dz) % NZL) * NR + (x + dx) % NR
        cols = pl.ds(pl.multiple_of(t * width, width), width)
        blocks = []
        for s in dense_slots(t):
            block = w_all[s, 2]
            blocks.append(jnp.concatenate([block[:, 128 * j : 128 * (j + 1)] for j in range(ff // 128)], axis=0))
        weights = jnp.concatenate([w_down[:, cols], jnp.concatenate(blocks, axis=1)], axis=0)
        return dot(hidden[g], weights)

    def rs_number(g, number):
        return RS + 9 * g + number

    def r1(g):
        for dz in (1, 0):
            rs_send[g, 3 * dz] = down(g, dz, 2).astype(BF16)
            send(rs_number(g, 4 * dz), rs_send.at[g, 3 * dz, pl.ds(0, HALF), :], rs_half.at[g, 2 * dz], at_x(1))
            send(
                rs_number(g, 4 * dz + 1),
                rs_send.at[g, 3 * dz, pl.ds(HALF, HALF), :],
                rs_half.at[g, 2 * dz + 1],
                at_x(-1),
            )

    def r2(g):
        for dz in (1, 0):
            part = down(g, dz, 1)
            arrived(rs_number(g, 4 * dz))
            rs_send[g, 3 * dz + 1, 0:HALF, :] = (part[0:HALF] + rs_half[g, 2 * dz].astype(F32)).astype(BF16)
            rs_send[g, 3 * dz + 1, HALF:CH, :] = part[HALF:CH].astype(BF16)
            send(rs_number(g, 4 * dz + 2), rs_send.at[g, 3 * dz + 1], rs_full.at[g, 2 * dz], at_x(1))
            part = down(g, dz, 3)
            arrived(rs_number(g, 4 * dz + 1))
            rs_send[g, 3 * dz + 2, 0:HALF, :] = part[0:HALF].astype(BF16)
            rs_send[g, 3 * dz + 2, HALF:CH, :] = (part[HALF:CH] + rs_half[g, 2 * dz + 1].astype(F32)).astype(BF16)
            send(rs_number(g, 4 * dz + 3), rs_send.at[g, 3 * dz + 2], rs_full.at[g, 2 * dz + 1], at_x(-1))

    def gathered(g, dz):
        part = down(g, dz, 0)
        arrived(rs_number(g, 4 * dz + 2))
        arrived(rs_number(g, 4 * dz + 3))
        return part + rs_full[g, 2 * dz].astype(F32) + rs_full[g, 2 * dz + 1].astype(F32)

    def r3(g):
        rs_send[g, 6] = gathered(g, 1).astype(BF16)
        send(rs_number(g, 8), rs_send.at[g, 6], rs_z.at[g], partner)

    def r4(g):
        total = gathered(g, 0)
        arrived(rs_number(g, 8))
        total = (total + rs_z[g].astype(F32)).astype(BF16)
        if g == 0:
            returned[0:PAIR, :] = total[0:PAIR]
            result[PAIR:CH, :] = total[PAIR:CH]
        else:
            result[g * CH : (g + 1) * CH, :] = total
        for dy in range(NR):
            n = g * NR + dy
            if n:
                span = pl.ds(n * PAIR, PAIR)
                send(RET + n, result.at[span, :], returned.at[span, :], at_chip(dy, g))

    a, b, c, d = 1, 3, 2, 0
    dense(a)
    r1(a)
    dense(b)
    r1(b)
    r2(a)
    dense(c)
    r1(c)
    r2(b)
    r3(a)
    dense(d)
    r1(d)
    r2(c)
    r3(b)
    r4(a)
    r2(d)
    r3(c)
    r4(b)
    r3(d)
    r4(c)
    r4(d)

    def column(b, k):
        row = info[b, k : k + 1, :]
        return jnp.sum(eye * row, axis=1, keepdims=True).astype(jnp.int32) - core * ROWS

    other = 1 - core
    own_cols = [column(core, k) for k in range(2)]
    other_cols = [column(other, k) for k in range(2)]
    part_send[...] = jnp.zeros_like(part_send)
    part_own[...] = tok[core].astype(F32)
    for g in (a, b, c, d):
        for dy in range(NR):
            if g * NR + dy:
                arrived(RET + g * NR + dy)
        rows = lax.broadcasted_iota(jnp.int32, (n_tok, CH), 1) + g * CH
        block = returned[g * CH : (g + 1) * CH, :]
        for cols, target in ((other_cols, part_send), (own_cols, part_own)):
            chosen = (cols[0] == rows).astype(F32) + (cols[1] == rows).astype(F32)
            target[...] += dot(chosen.astype(BF16), block)
    send(SIB, part_send, part_recv, sibling)
    arrived(SIB)
    out[...] = (part_own[...] + part_recv[...]).astype(BF16)

    for copy in sent.values():
        copy.wait_send()


def body(tokens, routes, combine, expert_slot, dense_gate, dense_up, dense_down, expert_gate, expert_up, expert_down):
    n_tok, width = tokens.shape
    depth, ff = expert_gate.shape[1:]
    piece = dense_gate.shape[0]
    any_spec = pl.BlockSpec(memory_space=pl.ANY)
    vmem = pl.BlockSpec(memory_space=pltpu.VMEM)
    n_slots = NZL * NR
    return pl.pallas_call(
        kernel,
        out_shape=jax.ShapeDtypeStruct((n_tok, width), BF16),
        in_specs=[any_spec, vmem, vmem, vmem] + [any_spec] * 6,
        out_specs=vmem,
        scratch_shapes=[
            pltpu.VMEM((2, n_tok, width), BF16),
            pltpu.VMEM((2, 8, n_tok), F32),
            pltpu.VMEM((NR * NR, 8, 128), F32),
            pltpu.VMEM((NR * NR, 8, 128), F32),
            pltpu.VMEM((ROWS, 128), F32),
            pltpu.VMEM((ROWS, 128), F32),
            pltpu.VMEM((depth, ff), BF16),
            pltpu.VMEM((depth, ff), BF16),
            pltpu.VMEM((ff, depth), BF16),
            pltpu.VMEM((2 * NR * NR, 3, piece, ff), BF16),
            pltpu.VMEM((ROWS, width), BF16),
            pltpu.VMEM((n_slots, ROWS, width), BF16),
            pltpu.VMEM((NR, CH, ff), F32),
            pltpu.VMEM((NR, CH, ff), F32),
            pltpu.VMEM((NR, CH, 2 * ff), BF16),
            pltpu.VMEM((NR, 7, CH, width), BF16),
            pltpu.VMEM((NR, 4, HALF, width), BF16),
            pltpu.VMEM((NR, 4, CH, width), BF16),
            pltpu.VMEM((NR, CH, width), BF16),
            pltpu.VMEM((ROWS, width), BF16),
            pltpu.VMEM((ROWS, width), BF16),
            pltpu.VMEM((n_tok, width), F32),
            pltpu.VMEM((n_tok, width), F32),
            pltpu.VMEM((n_tok, width), F32),
            pltpu.SemaphoreType.DMA((N_SEM,)),
            pltpu.SemaphoreType.DMA((N_SEM,)),
            pltpu.SemaphoreType.DMA((9,)),
        ],
        compiler_params=pltpu.CompilerParams(
            collective_id=0, has_side_effects=True, vmem_limit_bytes=60 * 1024 * 1024
        ),
    )(
        tokens,
        routes,
        combine,
        expert_slot.reshape(1, -1),
        dense_gate,
        dense_up,
        dense_down,
        expert_gate,
        expert_up,
        expert_down,
    )


def solution(mesh):
    in_specs = (
        P("ep", "tp"),
        P("ep", None),
        P("ep", None),
        P(),
        P("ep", "tp"),
        P("ep", "tp"),
        P("tp", "ep"),
        P("ep", None, "tp"),
        P("ep", None, "tp"),
        P("ep", "tp", None),
    )
    out_specs = P("ep", "tp")
    return jax.shard_map(body, mesh=mesh, in_specs=in_specs, out_specs=out_specs, check_vma=False)
```

time: 468 us -> 182 us (0.39)
  waiting for transfers between devices: 368 us -> 0 us
  Pallas kernels: 0 us -> 174 us
  matrix products: 27.9 us -> 0 us
  starting transfers between devices: 25.3 us -> 0 us
  local copies, waits for them, and re-layouts: 26.1 us -> 4.5 us
  between operations: 13.6 us -> 0.01 us
  other arithmetic: 5.67 us -> 0 us
    pallas_call x0 -> x1, Pallas kernels: none -> 174 us  [body(): pl.pallas_call(kernel, out_shape=jax.ShapeDtypeStruct((n_tok, width), BF1...]
    all_to_all x2 -> x0, waiting for transfers between devices: 152 us -> none  [the longest x1 123 us: body(): lax.all_to_all(outgoing, 'ep', split_axis=0, concat_axis=0, tiled=True)]
    all_gather x4 -> x0, waiting for transfers between devices: 141 us -> none  [the longest x1 59.9 us: body(): lax.all_gather(dense_down, 'ep', axis=1, tiled=True)]
    reduce_scatter x2 -> x0, waiting for transfers between devices: 72.2 us -> none  [the longest x1 69.2 us: body(): lax.psum_scatter(expert_terms.astype(jnp.bfloat16), 'tp', scatter_dimensi...]
    dot_general x5 -> x0, matrix products: 27.9 us -> none  [the longest x1 6.57 us: body(): expert_g = jnp.dot(arrived, gate_w, preferred_element_type=jnp.float32)]
    all_to_all x2 -> x0, starting transfers between devices: 25 us -> none  [the longest x1 15.6 us: body(): lax.all_to_all(outgoing, 'ep', split_axis=0, concat_axis=0, tiled=True)]
    gather x2 -> x0, local copies, waits for them, and re-layouts: 16.9 us -> none  [the longest x1 13.6 us: body(): outgoing = source[table].reshape(n_ep, capacity, width)]
  transfers between devices with their start and end apart: 8 -> 0, of which waited for: 7 -> 0; matrix products, arithmetic and copies ran while one was open for 12% -> 0% of each run, Pallas kernels for 0% -> 0%
where the time goes in v1:
time: 182 us; the launch traced here: 179 us
  Pallas kernels  174 us (96%)
  local copies, waits for them, and re-layouts  4.5 us (2%)
    pallas_call x1, Pallas kernels, body(): pl.pallas_call(kernel, out_shape=jax.ShapeDtypeStruct((n_tok, width), BF1...  174 us
    unnamed x3, local copies, waits for them, and re-layouts  4.5 us

profile of v1, /device:TPU:1, one launch (start us, length us, event | category | flops | bytes accessed | tf_op | source)
XLA Modules:
  0.0 178.7 jit_solution(13450692726395865489)
XLA Ops:
  0.0 1.4 copy.11.routes
  1.4 1.4 copy.12.combine
  2.9 174.2 %shard_map.100 = bf16[192,512]{1,0:T(8,128)(2,1)} custom-call(bf16[192,512]{1,0:T(8,128)(2,1)} %tokens.1, s32[192,2]{1,0:T(8,128)} %copy.11.routes, f32[192,2]{1,0:T(8,128)} %copy.12.combine, s32[1,32]{1,0:T(1,128)} %bitcast.1, bf16[128,384]{1,0:T(8,128)(2,1)} %dense_gate.1, bf16[128,384]{1,0:T(8,128)(2,1)} %dense_up.1, bf16[384,128]{1,0:T(8,128)(2,1)} %dense_down.1, ...), custom_call_target="tpu_custom_call" | custom-call | tf_op jit(solution)/shard_map/pallas_call | solution.py:509
  177.1 1.6 copy.14

commit v2 on v1

--- a/solution.py
+++ b/solution.py
@@ -74,6 +74,7 @@
     load_sem,
 ):
     n_tok, width = tokens.shape
+    n_slot = slots.shape[1]
     ff = w_gate.shape[1]
     piece = dense_gate.shape[0]
     tp = lax.axis_index("tp")
@@ -130,27 +131,22 @@
     for peer in peers:
         pl.semaphore_signal(barrier, inc=1, device_id=peer, device_id_type=MESH)
 
-    route = routes[...]
-    lanes = lax.broadcasted_iota(jnp.int32, (n_tok, slots.shape[1]), 1)
-    picks = [(route[:, k : k + 1] == lanes).astype(F32) for k in range(2)]
+    experts = lax.broadcasted_iota(jnp.int32, (n_slot, n_tok), 0)
+    picks = [(routes[k : k + 1, :] == experts).astype(F32) for k in range(2)]
     row_id = lax.broadcasted_iota(jnp.int32, (n_tok, n_tok), 0)
     col_id = lax.broadcasted_iota(jnp.int32, (n_tok, n_tok), 1)
-    before = (col_id < row_id).astype(BF16)
-    eye = (col_id == row_id).astype(F32)
-    earlier = dot(before, (picks[0] + picks[1]).astype(BF16))
-    slot_row = slots[...].astype(F32)
-    columns = []
+    before = (row_id < col_id).astype(BF16)
+    earlier = dot((picks[0] + picks[1]).astype(BF16), before)
+    same = lax.broadcasted_iota(jnp.int32, (n_slot, n_slot), 0) == lax.broadcasted_iota(jnp.int32, (n_slot, n_slot), 1)
+    slot_of = jnp.sum(jnp.where(same, slots[...].astype(F32), 0.0), axis=1, keepdims=True)
     for k in range(2):
-        pos = jnp.sum(picks[k] * earlier, axis=1, keepdims=True).astype(jnp.int32)
-        dest = jnp.sum(picks[k] * slot_row, axis=1, keepdims=True).astype(jnp.int32)
+        pos = jnp.sum(picks[k] * earlier, axis=0, keepdims=True).astype(jnp.int32)
+        dest = jnp.sum(picks[k] * slot_of, axis=0, keepdims=True).astype(jnp.int32)
         rel_z = (zh - ((dest >> 1) & (NR - 1)) + NR) & (NR - 1)
         rel_y = (y - (dest >> 3) + NR) & (NR - 1)
         place = (dest & 1) * ROWS + (rel_z * NR + rel_y) * PAIR + core * CAP + pos
-        columns.append(place.astype(F32))
-    for k in range(2):
-        columns.append(combine[:, k : k + 1])
-    for number, column in enumerate(columns):
-        info[core, number : number + 1, :] = jnp.sum(eye * column, axis=0, keepdims=True)
+        info[core, k : k + 1, :] = place.astype(F32)
+        info[core, 2 + k : 3 + k, :] = combine[k : k + 1, :]
 
     pl.semaphore_wait(barrier, len(peers))
     loads[0].wait()
@@ -179,52 +175,35 @@
     def w_sibling(dz, dy):
         w_send(WS + dz * NR + dy, w_slot(dz, dy, 0), w_slot(dz, dy, 1), sibling)
 
-    def w_across(dz):
-        arrived(WY + 4 * dz)
-        w_send(WY + 4 * dz + 2, w_slot(dz, 3, 0), w_slot(dz, 2, 0), at_chip(1, 0), 0)
-        arrived(WY + 4 * dz + 1)
-        w_send(WY + 4 * dz + 3, w_slot(dz, 1, 0), w_slot(dz, 2, 0), at_chip(-1, 0), 1)
-        w_sibling(dz, 3)
-        w_sibling(dz, 1)
+    def w_across(dz, back):
+        dy = 1 if back else 3
+        arrived(WY + 4 * dz + back)
+        w_send(WY + 4 * dz + 2 + back, w_slot(dz, dy, 0), w_slot(dz, 2, 0), at_chip(1 - 2 * back, 0), back)
+        w_sibling(dz, dy)
 
     def w_last(dz):
         arrived(WY + 4 * dz + 2)
         arrived(WY + 4 * dz + 3)
         w_sibling(dz, 2)
 
-    def w0():
-        w_spread(0)
+    def w_start():
         w_send(WZ, w_slot(0, 0, 0), w_slot(3, 0, 0), at_chip(0, 1))
         w_send(WZ + 1, w_slot(0, 0, 0), w_slot(1, 0, 0), at_chip(0, -1))
         w_sibling(0, 0)
 
-    def w1():
-        arrived(WZ)
-        w_send(WZ + 2, w_slot(3, 0, 0), w_slot(2, 0, 0), at_chip(0, 1), 0)
-        arrived(WZ + 1)
-        w_send(WZ + 3, w_slot(1, 0, 0), w_slot(2, 0, 0), at_chip(0, -1), 1)
-        w_spread(3)
-        w_spread(1)
-        w_sibling(3, 0)
-        w_sibling(1, 0)
-        w_across(0)
-
-    def w2():
+    def w_next(dz):
+        arrived(WZ + (0 if dz == 3 else 1))
+        w_spread(dz)
+        w_sibling(dz, 0)
+
+    def w_half(back):
+        w_send(WZ + 2 + back, w_slot(1 if back else 3, 0, 0), w_slot(2, 0, 0), at_chip(0, 1 - 2 * back), back)
+
+    def w_far():
         arrived(WZ + 2)
         arrived(WZ + 3)
         w_spread(2)
         w_sibling(2, 0)
-        w_last(0)
-        w_across(3)
-        w_across(1)
-
-    def w3():
-        w_across(2)
-        w_last(3)
-        w_last(1)
-
-    def w4():
-        w_last(2)
 
     def w5():
         for number in range(NR * NR):
@@ -248,7 +227,7 @@
         first = zero_row + (1.0 - k)
         tables.append(jnp.concatenate([high, middle, low, first] + [zero_row] * 4, axis=0).astype(BF16))
 
-    for g in range(NR):
+    def pack(g):
         rows = lax.broadcasted_iota(jnp.int32, (CH, 2 * n_tok), 0) + g * CH
         picks = [(place[k] == rows).astype(F32) for k in range(2)]
         block = dot((picks[0] + picks[1]).astype(BF16), both).astype(BF16)
@@ -265,14 +244,14 @@
             outgoing[PAIR:CH, :] = block[PAIR:CH]
         else:
             outgoing[g * CH : (g + 1) * CH, :] = block
+
+    def dispatch(g):
         for dy in range(NR):
             n = g * NR + dy
             if n:
                 span = pl.ds(n * PAIR, PAIR)
                 send(A2A + n, outgoing.at[span, :], x_all.at[0, span, :], at_chip(-dy, -g))
                 send(META + n, meta_out.at[n], meta_in.at[n], at_chip(-dy, -g))
-
-    w0()
 
     def ag_send(g, number, slot, target, device, half=None):
         if half is None:
@@ -292,20 +271,18 @@
         ag_send(g, 1, 0, 3, at_x(1))
         ag_send(g, 2, 0, 1, at_x(-1))
 
-    def s2(g):
+    def s2b(g):
         ag_arrived(g, 0)
         ag_send(g, 3, 4, 7, at_x(1))
         ag_send(g, 4, 4, 5, at_x(-1))
-        ag_arrived(g, 1)
-        ag_send(g, 5, 3, 2, at_x(1), 0)
-        ag_arrived(g, 2)
-        ag_send(g, 6, 1, 2, at_x(-1), 1)
-
-    def s3(g):
-        ag_arrived(g, 3)
-        ag_send(g, 7, 7, 6, at_x(1), 0)
-        ag_arrived(g, 4)
-        ag_send(g, 8, 5, 6, at_x(-1), 1)
+
+    def s2a(g, back):
+        ag_arrived(g, 1 + back)
+        ag_send(g, 5 + back, 1 if back else 3, 2, at_x(1 - 2 * back), back)
+
+    def s3(g, back):
+        ag_arrived(g, 3 + back)
+        ag_send(g, 7 + back, 5 if back else 7, 6, at_x(1 - 2 * back), back)
 
     def tp_of(slot):
         return ((zl + slot // NR) % NZL) * NR + (x + slot % NR) % NR
@@ -364,31 +341,6 @@
                 column = jnp.sum(jnp.where(pick, row, 0.0), axis=1, keepdims=True)
                 target[n * PAIR : (n + 1) * PAIR, :] = jnp.broadcast_to(column, (PAIR, 128))
 
-    s1(0)
-    s1(1)
-    s2(0)
-    w1()
-    s1(3)
-    s2(1)
-    s3(0)
-    scales()
-    for copy in loads[n_dense:]:
-        copy.wait()
-    w2()
-    s1(2)
-    s2(3)
-    s3(1)
-    s4(0)
-    w3()
-    s2(2)
-    s3(3)
-    s4(1)
-    w4()
-    s3(2)
-    s4(3)
-    s4(2)
-    w5()
-
     def down(g, dz, dx):
         t = ((zl + dz) % NZL) * NR + (x + dx) % NR
         cols = pl.ds(pl.multiple_of(t * width, width), width)
@@ -402,29 +354,23 @@
     def rs_number(g, number):
         return RS + 9 * g + number
 
-    def r1(g):
-        for dz in (1, 0):
-            rs_send[g, 3 * dz] = down(g, dz, 2).astype(BF16)
-            send(rs_number(g, 4 * dz), rs_send.at[g, 3 * dz, pl.ds(0, HALF), :], rs_half.at[g, 2 * dz], at_x(1))
-            send(
-                rs_number(g, 4 * dz + 1),
-                rs_send.at[g, 3 * dz, pl.ds(HALF, HALF), :],
-                rs_half.at[g, 2 * dz + 1],
-                at_x(-1),
-            )
-
-    def r2(g):
-        for dz in (1, 0):
-            part = down(g, dz, 1)
-            arrived(rs_number(g, 4 * dz))
-            rs_send[g, 3 * dz + 1, 0:HALF, :] = (part[0:HALF] + rs_half[g, 2 * dz].astype(F32)).astype(BF16)
-            rs_send[g, 3 * dz + 1, HALF:CH, :] = part[HALF:CH].astype(BF16)
-            send(rs_number(g, 4 * dz + 2), rs_send.at[g, 3 * dz + 1], rs_full.at[g, 2 * dz], at_x(1))
-            part = down(g, dz, 3)
-            arrived(rs_number(g, 4 * dz + 1))
-            rs_send[g, 3 * dz + 2, 0:HALF, :] = part[0:HALF].astype(BF16)
-            rs_send[g, 3 * dz + 2, HALF:CH, :] = (part[HALF:CH] + rs_half[g, 2 * dz + 1].astype(F32)).astype(BF16)
-            send(rs_number(g, 4 * dz + 3), rs_send.at[g, 3 * dz + 2], rs_full.at[g, 2 * dz + 1], at_x(-1))
+    def r1(g, dz):
+        rs_send[g, 3 * dz] = down(g, dz, 2).astype(BF16)
+        for back in range(2):
+            rows = pl.ds(back * HALF, HALF)
+            target = rs_half.at[g, 2 * dz + back]
+            send(rs_number(g, 4 * dz + back), rs_send.at[g, 3 * dz, rows, :], target, at_x(1 - 2 * back))
+
+    def r2(g, dz, back):
+        part = down(g, dz, 3 if back else 1)
+        arrived(rs_number(g, 4 * dz + back))
+        slot = 3 * dz + 1 + back
+        near, far = back * HALF, (1 - back) * HALF
+        both_rows = part[near : near + HALF] + rs_half[g, 2 * dz + back].astype(F32)
+        rs_send[g, slot, near : near + HALF, :] = both_rows.astype(BF16)
+        rs_send[g, slot, far : far + HALF, :] = part[far : far + HALF].astype(BF16)
+        target = rs_full.at[g, 2 * dz + back]
+        send(rs_number(g, 4 * dz + 2 + back), rs_send.at[g, slot], target, at_x(1 - 2 * back))
 
     def gathered(g, dz):
         part = down(g, dz, 0)
@@ -451,38 +397,18 @@
                 span = pl.ds(n * PAIR, PAIR)
                 send(RET + n, result.at[span, :], returned.at[span, :], at_chip(dy, g))
 
-    a, b, c, d = 1, 3, 2, 0
-    dense(a)
-    r1(a)
-    dense(b)
-    r1(b)
-    r2(a)
-    dense(c)
-    r1(c)
-    r2(b)
-    r3(a)
-    dense(d)
-    r1(d)
-    r2(c)
-    r3(b)
-    r4(a)
-    r2(d)
-    r3(c)
-    r4(b)
-    r3(d)
-    r4(c)
-    r4(d)
+    eye = (col_id == row_id).astype(F32)
 
     def column(b, k):
         row = info[b, k : k + 1, :]
         return jnp.sum(eye * row, axis=1, keepdims=True).astype(jnp.int32) - core * ROWS
 
-    other = 1 - core
     own_cols = [column(core, k) for k in range(2)]
-    other_cols = [column(other, k) for k in range(2)]
+    other_cols = [column(1 - core, k) for k in range(2)]
     part_send[...] = jnp.zeros_like(part_send)
     part_own[...] = tok[core].astype(F32)
-    for g in (a, b, c, d):
+
+    def combine_rows(g):
         for dy in range(NR):
             if g * NR + dy:
                 arrived(RET + g * NR + dy)
@@ -491,9 +417,112 @@
         for cols, target in ((other_cols, part_send), (own_cols, part_own)):
             chosen = (cols[0] == rows).astype(F32) + (cols[1] == rows).astype(F32)
             target[...] += dot(chosen.astype(BF16), block)
-    send(SIB, part_send, part_recv, sibling)
-    arrived(SIB)
-    out[...] = (part_own[...] + part_recv[...]).astype(BF16)
+
+    def exchange():
+        send(SIB, part_send, part_recv, sibling)
+        arrived(SIB)
+        out[...] = (part_own[...] + part_recv[...]).astype(BF16)
+
+    w_start()
+    pack(3)
+    pack(0)
+    pack(1)
+    dispatch(0)
+    w_spread(0)
+    dispatch(1)
+    s1(0)
+    dispatch(3)
+    s2a(0, 0)
+    s2a(0, 1)
+    s1(3)
+    w_next(3)
+    w_across(0, 0)
+    w_next(1)
+    pack(2)
+    s1(1)
+    s2b(0)
+    s2b(3)
+    dispatch(2)
+    w_across(3, 1)
+    s2b(1)
+    w_across(0, 1)
+    s3(3, 0)
+    s3(3, 1)
+    s2a(1, 1)
+    w_across(1, 1)
+    s3(0, 0)
+    w_half(1)
+    w_half(0)
+    w_across(3, 0)
+    s2a(3, 0)
+    s2a(3, 1)
+    w_across(1, 0)
+    scales()
+    w_far()
+    s1(2)
+    for copy in loads[n_dense:]:
+        copy.wait()
+    s4(3)
+    s3(1, 0)
+    s3(0, 1)
+    s2a(2, 0)
+    s2b(2)
+    w_across(2, 0)
+    w_across(2, 1)
+    w_last(3)
+    w_last(1)
+    s4(0)
+    w_last(0)
+    s3(1, 1)
+    w_last(2)
+    s2a(2, 1)
+    s2a(1, 0)
+    s3(2, 1)
+    w5()
+    s3(2, 0)
+    dense(3)
+    r1(3, 1)
+    r1(3, 0)
+    s4(1)
+    dense(1)
+    r1(1, 0)
+    r2(3, 1, 0)
+    r1(1, 1)
+    r2(3, 1, 1)
+    s4(2)
+    dense(0)
+    r2(1, 1, 1)
+    r2(1, 1, 0)
+    r3(3)
+    r2(1, 0, 0)
+    r2(1, 0, 1)
+    dense(2)
+    r3(1)
+    r2(3, 0, 0)
+    r1(2, 1)
+    r2(3, 0, 1)
+    r4(1)
+    r1(0, 1)
+    r2(2, 1, 1)
+    r2(2, 1, 0)
+    r4(3)
+    r1(2, 0)
+    r2(0, 1, 1)
+    r2(0, 1, 0)
+    r3(2)
+    r2(2, 0, 0)
+    r1(0, 0)
+    r2(2, 0, 1)
+    combine_rows(1)
+    r3(0)
+    r2(0, 0, 0)
+    r4(2)
+    r2(0, 0, 1)
+    combine_rows(3)
+    r4(0)
+    combine_rows(0)
+    combine_rows(2)
+    exchange()
 
     for copy in sent.values():
         copy.wait_send()
@@ -545,8 +574,8 @@
         ),
     )(
         tokens,
-        routes,
-        combine,
+        routes.T,
+        combine.T,
         expert_slot.reshape(1, -1),
         dense_gate,
         dense_up,

time: 182 us -> 164 us (0.901); the launches traced: 179 us -> 163 us
  Pallas kernels: 174 us -> 162 us
  local copies, waits for them, and re-layouts: 4.5 us -> 1.62 us
    pallas_call x1, Pallas kernels: 174 us -> 162 us  [body(): pl.pallas_call(kernel, out_shape=jax.ShapeDtypeStruct((n_tok, width), BF1...]
    unnamed x3 -> x1, local copies, waits for them, and re-layouts: 4.5 us -> 1.62 us
where the time goes in v2:
time: 164 us; the launch traced here: 163 us
  Pallas kernels  162 us (99%)
    pallas_call x1, Pallas kernels, body(): pl.pallas_call(kernel, out_shape=jax.ShapeDtypeStruct((n_tok, width), BF1...  162 us

profile of v2, /device:TPU:1, one launch (start us, length us, event | category | flops | bytes accessed | tf_op | source)
XLA Modules:
  0.0 163.1 jit_solution(11025425238463342412)
XLA Ops:
  0.0 161.5 %shard_map.100 = bf16[192,512]{1,0:T(8,128)(2,1)} custom-call(bf16[192,512]{1,0:T(8,128)(2,1)} %tokens.1, s32[2,192]{1,0:T(2,128)} %bitcast.3, f32[2,192]{1,0:T(2,128)} %bitcast.4, s32[1,32]{1,0:T(1,128)} %bitcast.5, bf16[128,384]{1,0:T(8,128)(2,1)} %dense_gate.1, bf16[128,384]{1,0:T(8,128)(2,1)} %dense_up.1, bf16[384,128]{1,0:T(8,128)(2,1)} %dense_down.1, ...), custom_call_target="tpu_custom_call" | custom-call | tf_op jit(solution)/shard_map/pallas_call | solution.py:538
  161.5 1.6 copy.12

commit v3 on v2

--- a/solution.py
+++ b/solution.py
@@ -16,9 +16,10 @@
 ROWS = NR * NR * PAIR
 CH = NR * PAIR
 HALF = CH // 2
-N_SEM = 160
-
-A2A, META, TOK, INFO, AG, WZ, WY, WS, RS, RET, SIB = 0, 16, 32, 33, 34, 70, 74, 90, 106, 142, 158
+BY_Z = (1, 2, 3)
+N_SEM = 164
+
+A2A, META, TOK, INFO, AG, WZ, WY, WS, RS, RET, SIB, FAR = 0, 16, 32, 33, 34, 70, 74, 90, 106, 142, 158, 160
 
 
 def dot(a, b):
@@ -57,13 +58,12 @@
     w_all,
     outgoing,
     x_all,
-    acc_g,
-    acc_u,
     hidden,
     rs_send,
     rs_half,
     rs_full,
     rs_z,
+    rs_far,
     result,
     returned,
     part_send,
@@ -284,9 +284,6 @@
         ag_arrived(g, 3 + back)
         ag_send(g, 7 + back, 5 if back else 7, 6, at_x(1 - 2 * back), back)
 
-    def tp_of(slot):
-        return ((zl + slot // NR) % NZL) * NR + (x + slot % NR) % NR
-
     def dense_slots(t):
         found = []
         for j in range(4):
@@ -297,37 +294,29 @@
             found.append(w_slot(dz, dy, dc))
         return found
 
+    def features(g):
+        parts = []
+        for t in range(NZL * NR):
+            slot = ((t // NR - zl + NZL) % NZL) * NR + (t % NR - x + NR) % NR
+            parts.append(x_all[slot, pl.ds(g * CH, CH), :])
+        return jnp.concatenate(parts, axis=1)
+
+    def activate(gate, up, scale, g):
+        spread = jnp.concatenate([scale[g * CH : (g + 1) * CH, :]] * (ff // 128), axis=1)
+        return (silu(gate) * up * spread).astype(BF16)
+
     def s4(g):
         for number in range(5, 9):
             ag_arrived(g, number)
-        acc_g[g] = jnp.zeros((CH, ff), F32)
-        acc_u[g] = jnp.zeros((CH, ff), F32)
-
-        def step(slot, _):
-            part = x_all[slot, pl.ds(g * CH, CH), :]
-            rows = pl.ds(pl.multiple_of(tp_of(slot) * width, width), width)
-            acc_g[g] += dot(part, w_gate[rows, :])
-            acc_u[g] += dot(part, w_up[rows, :])
-            return 0
-
-        lax.fori_loop(0, NZL * NR, step, 0)
-        spread = jnp.concatenate([scale_e[g * CH : (g + 1) * CH, :]] * (ff // 128), axis=1)
-        hidden[g, :, 0:ff] = (silu(acc_g[g]) * acc_u[g] * spread).astype(BF16)
+        rows = features(g)
+        hidden[g, :, 0:ff] = activate(dot(rows, w_gate[...]), dot(rows, w_up[...]), scale_e, g)
 
     def dense(g):
-        acc_g[g] = jnp.zeros((CH, ff), F32)
-        acc_u[g] = jnp.zeros((CH, ff), F32)
-
-        def step(slot, _):
-            part = x_all[slot, pl.ds(g * CH, CH), :]
-            found = dense_slots(tp_of(slot))
-            acc_g[g] += dot(part, jnp.concatenate([w_all[s, 0] for s in found], axis=0))
-            acc_u[g] += dot(part, jnp.concatenate([w_all[s, 1] for s in found], axis=0))
-            return 0
-
-        lax.fori_loop(0, NZL * NR, step, 0)
-        spread = jnp.concatenate([scale_d[g * CH : (g + 1) * CH, :]] * (ff // 128), axis=1)
-        hidden[g, :, ff : 2 * ff] = (silu(acc_g[g]) * acc_u[g] * spread).astype(BF16)
+        rows = features(g)
+        order = [s for t in range(NZL * NR) for s in dense_slots(t)]
+        gate = dot(rows, jnp.concatenate([w_all[s, 0] for s in order], axis=0))
+        up = dot(rows, jnp.concatenate([w_all[s, 1] for s in order], axis=0))
+        hidden[g, :, ff : 2 * ff] = activate(gate, up, scale_d, g)
 
     def scales():
         pick = lax.broadcasted_iota(jnp.int32, (PAIR, 128), 0) == lax.broadcasted_iota(jnp.int32, (PAIR, 128), 1)
@@ -354,8 +343,16 @@
     def rs_number(g, number):
         return RS + 9 * g + number
 
+    def rz(g):
+        rs_send[g, 3] = down(g, 1, 2).astype(BF16)
+        send(FAR + g, rs_send.at[g, 3], rs_far.at[g], partner)
+
     def r1(g, dz):
-        rs_send[g, 3 * dz] = down(g, dz, 2).astype(BF16)
+        part = down(g, dz, 2)
+        if dz == 0 and g in BY_Z:
+            arrived(FAR + g)
+            part = part + rs_far[g].astype(F32)
+        rs_send[g, 3 * dz] = part.astype(BF16)
         for back in range(2):
             rows = pl.ds(back * HALF, HALF)
             target = rs_half.at[g, 2 * dz + back]
@@ -363,12 +360,15 @@
 
     def r2(g, dz, back):
         part = down(g, dz, 3 if back else 1)
-        arrived(rs_number(g, 4 * dz + back))
         slot = 3 * dz + 1 + back
-        near, far = back * HALF, (1 - back) * HALF
-        both_rows = part[near : near + HALF] + rs_half[g, 2 * dz + back].astype(F32)
-        rs_send[g, slot, near : near + HALF, :] = both_rows.astype(BF16)
-        rs_send[g, slot, far : far + HALF, :] = part[far : far + HALF].astype(BF16)
+        if dz == 1 and g in BY_Z:
+            rs_send[g, slot] = part.astype(BF16)
+        else:
+            arrived(rs_number(g, 4 * dz + back))
+            near, far = back * HALF, (1 - back) * HALF
+            both_rows = part[near : near + HALF] + rs_half[g, 2 * dz + back].astype(F32)
+            rs_send[g, slot, near : near + HALF, :] = both_rows.astype(BF16)
+            rs_send[g, slot, far : far + HALF, :] = part[far : far + HALF].astype(BF16)
         target = rs_full.at[g, 2 * dz + back]
         send(rs_number(g, 4 * dz + 2 + back), rs_send.at[g, slot], target, at_x(1 - 2 * back))
 
@@ -424,104 +424,104 @@
         out[...] = (part_own[...] + part_recv[...]).astype(BF16)
 
     w_start()
-    pack(3)
+    w_spread(0)
     pack(0)
     pack(1)
+    pack(3)
     dispatch(0)
-    w_spread(0)
     dispatch(1)
+    w_across(0, 0)
     s1(0)
     dispatch(3)
+    s1(1)
+    s2a(0, 1)
+    w_next(3)
     s2a(0, 0)
-    s2a(0, 1)
     s1(3)
-    w_next(3)
-    w_across(0, 0)
+    s2a(1, 1)
+    s2a(1, 0)
+    w_across(3, 0)
     w_next(1)
+    s2b(0)
+    w_half(0)
+    w_half(1)
+    w_across(0, 1)
+    w_across(1, 1)
+    s2b(1)
+    s3(0, 1)
+    w_across(3, 1)
     pack(2)
-    s1(1)
-    s2b(0)
+    s2a(3, 1)
+    dispatch(2)
+    s3(0, 0)
+    w_across(1, 0)
+    scales()
     s2b(3)
-    dispatch(2)
-    w_across(3, 1)
-    s2b(1)
-    w_across(0, 1)
+    s3(1, 0)
+    w_far()
+    for copy in loads[n_dense:]:
+        copy.wait()
+    s4(0)
+    s2a(3, 0)
+    s3(1, 1)
     s3(3, 0)
     s3(3, 1)
-    s2a(1, 1)
-    w_across(1, 1)
-    s3(0, 0)
-    w_half(1)
-    w_half(0)
-    w_across(3, 0)
-    s2a(3, 0)
-    s2a(3, 1)
-    w_across(1, 0)
-    scales()
-    w_far()
+    w_last(3)
+    w_last(1)
+    w_last(0)
     s1(2)
-    for copy in loads[n_dense:]:
-        copy.wait()
-    s4(3)
-    s3(1, 0)
-    s3(0, 1)
-    s2a(2, 0)
-    s2b(2)
     w_across(2, 0)
     w_across(2, 1)
-    w_last(3)
-    w_last(1)
-    s4(0)
-    w_last(0)
-    s3(1, 1)
+    s4(1)
     w_last(2)
+    s2b(2)
+    w5()
+    dense(1)
+    s2a(2, 0)
     s2a(2, 1)
-    s2a(1, 0)
+    rz(1)
+    s3(2, 0)
     s3(2, 1)
-    w5()
-    s3(2, 0)
-    dense(3)
-    r1(3, 1)
-    r1(3, 0)
-    s4(1)
-    dense(1)
-    r1(1, 0)
-    r2(3, 1, 0)
-    r1(1, 1)
-    r2(3, 1, 1)
-    s4(2)
     dense(0)
+    r1(0, 1)
     r2(1, 1, 1)
     r2(1, 1, 0)
+    s4(2)
+    dense(2)
+    r2(2, 1, 0)
+    r2(2, 1, 1)
+    rz(2)
+    r2(0, 1, 0)
+    r2(0, 1, 1)
+    s4(3)
+    r3(1)
+    r1(2, 0)
+    dense(3)
+    rz(3)
+    r2(3, 1, 0)
+    r2(3, 1, 1)
+    r3(2)
+    r2(2, 0, 1)
+    r2(2, 0, 0)
+    r1(1, 0)
+    r3(0)
+    r1(3, 0)
     r3(3)
     r2(1, 0, 0)
     r2(1, 0, 1)
-    dense(2)
-    r3(1)
+    r4(2)
     r2(3, 0, 0)
-    r1(2, 1)
+    r1(0, 0)
     r2(3, 0, 1)
+    r2(0, 0, 0)
     r4(1)
-    r1(0, 1)
-    r2(2, 1, 1)
-    r2(2, 1, 0)
+    r2(0, 0, 1)
     r4(3)
-    r1(2, 0)
-    r2(0, 1, 1)
-    r2(0, 1, 0)
-    r3(2)
-    r2(2, 0, 0)
-    r1(0, 0)
-    r2(2, 0, 1)
+    combine_rows(2)
+    r4(0)
     combine_rows(1)
-    r3(0)
-    r2(0, 0, 0)
-    r4(2)
-    r2(0, 0, 1)
+    combine_rows(0)
     combine_rows(3)
-    r4(0)
-    combine_rows(0)
-    combine_rows(2)
     exchange()
 
     for copy in sent.values():
@@ -553,12 +553,11 @@
             pltpu.VMEM((2 * NR * NR, 3, piece, ff), BF16),
             pltpu.VMEM((ROWS, width), BF16),
             pltpu.VMEM((n_slots, ROWS, width), BF16),
-            pltpu.VMEM((NR, CH, ff), F32),
-            pltpu.VMEM((NR, CH, ff), F32),
             pltpu.VMEM((NR, CH, 2 * ff), BF16),
             pltpu.VMEM((NR, 7, CH, width), BF16),
             pltpu.VMEM((NR, 4, HALF, width), BF16),
             pltpu.VMEM((NR, 4, CH, width), BF16),
+            pltpu.VMEM((NR, CH, width), BF16),
             pltpu.VMEM((NR, CH, width), BF16),
             pltpu.VMEM((ROWS, width), BF16),
             pltpu.VMEM((ROWS, width), BF16),

time: 164 us -> 155 us (0.945)
  Pallas kernels: 162 us -> 153 us
    pallas_call x1, Pallas kernels: 162 us -> 153 us  [body(): pl.pallas_call(kernel, out_shape=jax.ShapeDtypeStruct((n_tok, width), BF1...]
where the time goes in v3:
time: 155 us
  Pallas kernels  153 us (99%)
  local copies, waits for them, and re-layouts  1.62 us (1%)
    pallas_call x1, Pallas kernels, body(): pl.pallas_call(kernel, out_shape=jax.ShapeDtypeStruct((n_tok, width), BF1...  153 us

profile of v3, /device:TPU:1, one launch (start us, length us, event | category | flops | bytes accessed | tf_op | source)
XLA Modules:
  0.0 154.9 jit_solution(4560379562386899850)
XLA Ops:
  0.0 153.3 %shard_map.100 = bf16[192,512]{1,0:T(8,128)(2,1)} custom-call(bf16[192,512]{1,0:T(8,128)(2,1)} %tokens.1, s32[2,192]{1,0:T(2,128)} %bitcast.3, f32[2,192]{1,0:T(2,128)} %bitcast.4, s32[1,32]{1,0:T(1,128)} %bitcast.5, bf16[128,384]{1,0:T(8,128)(2,1)} %dense_gate.1, bf16[128,384]{1,0:T(8,128)(2,1)} %dense_up.1, bf16[384,128]{1,0:T(8,128)(2,1)} %dense_down.1, ...), custom_call_target="tpu_custom_call" | custom-call | tf_op jit(solution)/shard_map/pallas_call | solution.py:538
  153.3 1.6 %copy.12 = bf16[192,512]{1,0:T(8,128)(2,1)} copy(bf16[192,512]{1,0:T(8,128)(2,1)} %shard_map.100) | data formatting | bytes 393216

commit v4 on v3

--- a/solution.py
+++ b/solution.py
@@ -16,7 +16,7 @@
 ROWS = NR * NR * PAIR
 CH = NR * PAIR
 HALF = CH // 2
-BY_Z = (1, 2, 3)
+BY_Z = (0, 1, 2, 3)
 N_SEM = 164
 
 A2A, META, TOK, INFO, AG, WZ, WY, WS, RS, RET, SIB, FAR = 0, 16, 32, 33, 34, 70, 74, 90, 106, 142, 158, 160
@@ -425,103 +425,103 @@
 
     w_start()
     w_spread(0)
-    pack(0)
     pack(1)
     pack(3)
+    pack(2)
+    pack(0)
+    dispatch(3)
     dispatch(0)
+    s1(0)
+    w_across(0, 1)
     dispatch(1)
-    w_across(0, 0)
-    s1(0)
-    dispatch(3)
-    s1(1)
     s2a(0, 1)
-    w_next(3)
     s2a(0, 0)
     s1(3)
-    s2a(1, 1)
-    s2a(1, 0)
-    w_across(3, 0)
     w_next(1)
+    s2a(3, 0)
+    s2a(3, 1)
+    w_next(3)
+    w_across(0, 0)
+    s1(1)
     s2b(0)
+    w_across(1, 1)
     w_half(0)
     w_half(1)
-    w_across(0, 1)
-    w_across(1, 1)
+    w_across(3, 1)
+    s2b(3)
+    w_across(3, 0)
+    s3(0, 0)
     s2b(1)
+    w_across(1, 0)
     s3(0, 1)
-    w_across(3, 1)
-    pack(2)
-    s2a(3, 1)
+    w_last(0)
     dispatch(2)
-    s3(0, 0)
-    w_across(1, 0)
     scales()
-    s2b(3)
-    s3(1, 0)
     w_far()
+    w_last(3)
+    s3(3, 1)
+    s3(3, 0)
     for copy in loads[n_dense:]:
         copy.wait()
     s4(0)
-    s2a(3, 0)
+    s3(1, 0)
+    s2a(1, 1)
     s3(1, 1)
-    s3(3, 0)
-    s3(3, 1)
-    w_last(3)
+    s2a(1, 0)
+    s4(3)
+    s1(2)
     w_last(1)
-    w_last(0)
-    s1(2)
+    w_across(2, 1)
     w_across(2, 0)
-    w_across(2, 1)
     s4(1)
+    s2b(2)
     w_last(2)
-    s2b(2)
     w5()
+    dense(3)
+    r2(3, 1, 1)
+    s2a(2, 1)
+    rz(3)
+    s2a(2, 0)
     dense(1)
-    s2a(2, 0)
-    s2a(2, 1)
-    rz(1)
     s3(2, 0)
     s3(2, 1)
     dense(0)
-    r1(0, 1)
-    r2(1, 1, 1)
-    r2(1, 1, 0)
+    rz(1)
+    r2(3, 1, 0)
+    r2(0, 1, 0)
+    rz(0)
+    r1(3, 0)
+    r2(0, 1, 1)
     s4(2)
     dense(2)
+    rz(2)
+    r2(2, 1, 1)
     r2(2, 1, 0)
-    r2(2, 1, 1)
-    rz(2)
-    r2(0, 1, 0)
-    r2(0, 1, 1)
-    s4(3)
-    r3(1)
+    r3(0)
+    r1(1, 0)
     r1(2, 0)
-    dense(3)
-    rz(3)
-    r2(3, 1, 0)
-    r2(3, 1, 1)
+    r3(3)
+    r2(1, 1, 0)
+    r2(1, 1, 1)
     r3(2)
     r2(2, 0, 1)
     r2(2, 0, 0)
-    r1(1, 0)
-    r3(0)
-    r1(3, 0)
-    r3(3)
+    r3(1)
+    r2(3, 0, 1)
+    r2(3, 0, 0)
+    r4(2)
+    r2(1, 0, 1)
+    r1(0, 0)
     r2(1, 0, 0)
-    r2(1, 0, 1)
-    r4(2)
-    r2(3, 0, 0)
-    r1(0, 0)
-    r2(3, 0, 1)
+    r2(0, 0, 1)
     r2(0, 0, 0)
+    r4(3)
     r4(1)
-    r2(0, 0, 1)
-    r4(3)
+    r4(0)
     combine_rows(2)
-    r4(0)
+    combine_rows(3)
+    combine_rows(0)
     combine_rows(1)
-    combine_rows(0)
-    combine_rows(3)
     exchange()
 
     for copy in sent.values():

time: 155 us -> 152 us (0.981)
  Pallas kernels: 153 us -> 151 us
    pallas_call x1, Pallas kernels: 153 us -> 151 us  [body(): pl.pallas_call(kernel, out_shape=jax.ShapeDtypeStruct((n_tok, width), BF1...]
where the time goes in v4:
time: 152 us
  Pallas kernels  151 us (99%)
  local copies, waits for them, and re-layouts  1.62 us (1%)
    pallas_call x1, Pallas kernels, body(): pl.pallas_call(kernel, out_shape=jax.ShapeDtypeStruct((n_tok, width), BF1...  151 us

profile of v4, /device:TPU:1, one launch (start us, length us, event | category | flops | bytes accessed | tf_op | source)
XLA Modules:
  0.0 152.3 jit_solution(12470884405301657068)
XLA Ops:
  0.0 150.7 %shard_map.100 = bf16[192,512]{1,0:T(8,128)(2,1)} custom-call(bf16[192,512]{1,0:T(8,128)(2,1)} %tokens.1, s32[2,192]{1,0:T(2,128)} %bitcast.3, f32[2,192]{1,0:T(2,128)} %bitcast.4, s32[1,32]{1,0:T(1,128)} %bitcast.5, bf16[128,384]{1,0:T(8,128)(2,1)} %dense_gate.1, bf16[128,384]{1,0:T(8,128)(2,1)} %dense_up.1, bf16[384,128]{1,0:T(8,128)(2,1)} %dense_down.1, ...), custom_call_target="tpu_custom_call" | custom-call | tf_op jit(solution)/shard_map/pallas_call | solution.py:538
  150.7 1.6 %copy.12 = bf16[192,512]{1,0:T(8,128)(2,1)} copy(bf16[192,512]{1,0:T(8,128)(2,1)} %shard_map.100) | data formatting | bytes 393216
